TPU v7x, 32 devices: a whole 2x2x4 slice. The times are simulated.
32 devices in a mesh: row: 8 (over z, core), col: 4 (over y, x).
Axes of the slice: x: 2, y: 2, z: 4, core: 2. Of those that a mesh axis runs over, the one named last changes fastest.
Arguments:
- features: bfloat16 [4096, 256], P(('col', 'row')), may hold values from -6 to 6
- source_scale: float32 [4096], P(('col', 'row')), may hold values from 0.1 to 1
- target_scale: float32 [8192], P('row'), may hold values from 0.1 to 1
- weight: bfloat16 [256, 256], replicated, may hold values from -0.375 to 0.375
- cotangent: bfloat16 [8192, 256], P(('row', 'col')), may hold values from -6 to 6
- tile_src: int32 [64, 4, 8], P('row', 'col'), may hold values from 0 to 7, as said below
- tile_count: int32 [64, 4], P('row', 'col'), may hold values from 1 to 8, as said below
- edge_tgt: int32 [64, 4, 8, 32], P('row', 'col'), may hold values from 0 to 127
- edge_src: int32 [64, 4, 8, 32], P('row', 'col'), may hold values from 0 to 127
Outputs:
- activated: bfloat16 [8192, 256], P(('row', 'col'))
- weight_grad: float32 [256, 256], replicated
- feature_grad: bfloat16 [4096, 256], P(('col', 'row'))
Inputs may be any that keep to these rules, and one draw needn't show every extreme that they name: `tile_src`: within one target block and one grid column the 8 slots name distinct source blocks of that column; slots at or past the block's count are unused. `tile_count`: some target block of some grid column uses all 8 slots in every draw.
All inputs are finite; a program needn't handle non-finite values.
Results may differ from a plain program's by a relative error of at most 0.018.
Values may be sent and summed in bfloat16 or wider, within the bound.
A program may use at most 64 MiB of HBM per device.

v0:
```python
import math

import jax
import jax.numpy as jnp
from jax import lax
from jax.sharding import PartitionSpec as P

B = 128


def densify(item):
    targets, sources, count = item
    places = lax.iota(jnp.int32, B)
    target_hot = (targets[:, :, None] == places).astype(jnp.bfloat16)
    source_hot = (sources[:, :, None] == places).astype(jnp.bfloat16)
    tile = jnp.einsum("jea,jeb->jab", target_hot, source_hot, preferred_element_type=jnp.float32)
    living = lax.iota(jnp.int32, targets.shape[0]) < count
    return jnp.where(living[:, None, None], tile, 0.0).astype(jnp.bfloat16)


def silu_parts(z_value):
    sigma = jax.nn.sigmoid(z_value)
    return ((z_value * sigma).astype(jnp.bfloat16), sigma * (1.0 + z_value * (1.0 - sigma)))


def on_device(
    features,
    source_scale,
    target_scale,
    weight,
    cotangent,
    tile_src,
    tile_count,
    edge_tgt,
    edge_src,
):
    width = features.shape[1]
    blocks = tile_src.shape[0]
    slots = tile_src[:, 0]
    tiles = lax.map(densify, (edge_tgt[:, 0], edge_src[:, 0], tile_count[:, 0]))
    scaled = (source_scale[:, None] * features.astype(jnp.float32)).astype(jnp.bfloat16)
    gathered = lax.all_gather(scaled, "row", axis=0, tiled=True).reshape(-1, B, width)
    picked = gathered[slots]
    partial_value = jnp.einsum(
        "tjab,tjbf->taf", tiles, picked, preferred_element_type=jnp.float32
    ).reshape(blocks * B, width)
    share_rows = cotangent.shape[0]
    offset = lax.axis_index("col") * share_rows
    summed = lax.psum_scatter(
        partial_value.astype(jnp.bfloat16), "col", scatter_dimension=0, tiled=True
    ).astype(jnp.float32)
    scale_share = lax.dynamic_slice_in_dim(target_scale, offset, share_rows)
    agg_share = (scale_share[:, None] * summed).astype(jnp.bfloat16)
    z_value = jnp.dot(agg_share, weight, preferred_element_type=jnp.float32)
    activated, deriv = silu_parts(z_value)
    grad_share = (cotangent.astype(jnp.float32) * deriv).astype(jnp.bfloat16)
    grad_y_share = (
        scale_share[:, None] * jnp.dot(grad_share, weight.T, preferred_element_type=jnp.float32)
    ).astype(jnp.bfloat16)
    grad_y = lax.all_gather(grad_y_share, "col", axis=0, tiled=True)
    local_grad = jnp.dot(agg_share.T, grad_share, preferred_element_type=jnp.float32)
    total_nodes = target_scale.shape[0] * lax.axis_size("row")
    weight_grad = lax.psum(local_grad, ("row", "col")) / math.sqrt(total_nodes)
    grad_blocks = grad_y.reshape(blocks, B, width)

    def back_step(carry, item):
        tile_now, slot_now, grad_now = item
        contrib = jnp.einsum("jab,af->jbf", tile_now, grad_now, preferred_element_type=jnp.float32)
        return (carry.at[slot_now].add(contrib), None)

    start = jnp.zeros((gathered.shape[0], B, width), jnp.float32)
    terms, unused = lax.scan(back_step, start, (tiles, slots, grad_blocks))
    rounded_terms = terms.reshape(-1, width).astype(jnp.bfloat16)
    owned = lax.psum_scatter(rounded_terms, "row", scatter_dimension=0, tiled=True).astype(
        jnp.float32
    )
    feature_grad = (source_scale[:, None] * owned).astype(jnp.bfloat16)
    return (activated, weight_grad, feature_grad)


def solution(mesh):
    in_specs = (
        P(("col", "row"), None),
        P(("col", "row")),
        P("row"),
        P(),
        P(("row", "col"), None),
        P("row", "col", None),
        P("row", "col"),
        P("row", "col", None, None),
        P("row", "col", None, None),
    )
    out_specs = (P(("row", "col"), None), P(), P(("col", "row"), None))
    return jax.shard_map(
        on_device, mesh=mesh, in_specs=in_specs, out_specs=out_specs, check_vma=False
    )
```

profile of v0, /device:TPU:0, one launch (start us, length us, event | category | flops | bytes accessed | tf_op | source)
XLA Modules:
  0.0 254.1 jit_solution(17239309337689965877)
XLA Ops:
  7.3 25.0 %while.20 = (s32[]{:T(128)}, bf16[8,8,128,128]{3,2,1,0:T(8,128)(2,1)S(1)}, s32[8]{0:T(128)}, s32[8,8,32]{2,1,0:T(8,128)}, s32[8,8,32]{2,1,0:T(8,128)}, /*index=5*/s32[]{:T(128)}) while((s32[]{:T(128)}, bf16[8,8,128,128]{3,2,1,0:T(8,128)(2,1)S(1)}, s32[8]{0:T(128)}, s32[8,8,32]{2,1,0:T(8,128)}, s32[8,8,32]{2,1,0:T(8,128)}, ...), condition=%wide.region_1.2_spmd, body=%wide.region_0.1_spmd.sunk | while | flops 8716298 | bytes 275053 | solution.py:40
  7.3 1.2 dynamic_slice.50
  10.4 1.2 dynamic_slice.50
  13.5 1.2 dynamic_slice.50
  29.1 1.2 dynamic_slice.50
  32.4 16.6 %all_gather.6 = bf16[1024,256]{1,0:T(8,128)(2,1)S(1)} all-gather(bf16[128,256]{1,0:T(8,128)(2,1)S(1)} %multiply_convert_fusion.4), channel_id=1, replica_groups=mesh['row'=8,'col'=4] {'row'}, dimensions={0}, use_global_device_ids=true | all-gather | bytes 589824 | tf_op jit(solution)/shard_map/all_gather | solution.py:42
  49.0 2.8 %gather_fusion = bf16[64,128,256]{2,1,0:T(8,128)(2,1)} fusion(bf16[8,128,256]{2,1,0:T(8,128)(2,1)S(1)} %bitcast.62, s32[1024]{0:T(1024)S(1)} %pad_clamp_fusion), kind=kCustom, calls=%fused_computation | custom fusion | bytes 8388864 | tf_op jit(solution)/shard_map/gather | solution.py:43
  51.8 3.9 %fusion.13 = bf16[8,128,256]{2,1,0:T(8,128)(2,1)} fusion(bf16[8,8,128,128]{3,2,1,0:T(8,128)(2,1)S(1)} %get-tuple-element.175, bf16[8,8,128,256]{3,2,1,0:T(8,128)(2,1)} %bitcast.63), kind=kOutput, calls=%fused_computation.24 | convolution fusion | flops 537133056 | bytes 6815744 | tf_op jit(solution)/shard_map/tjab,tjbf->taf/dot_general | solution.py:44
  56.5 25.2 %reduce-scatter.3.cloned.1.call-done = bf16[256,256]{1,0:T(8,128)(2,1)} async-done(((bf16[1024,256]{1,0:T(8,128)(2,1)}), bf16[256,256]{1,0:T(8,128)(2,1)}) %reduce-scatter.3.cloned.1.call-update) | async-done | bytes 131088 | tf_op jit(solution)/shard_map/reduce_scatter | solution.py:49
  81.7 2.0 multiply_convert_fusion
  85.0 10.0 %all_gather.7 = bf16[1024,256]{1,0:T(8,128)(2,1)S(1)} all-gather(bf16[256,256]{1,0:T(8,128)(2,1)S(1)} %fusion.14), channel_id=1, replica_groups=mesh['row'=8,'col'=4] {'col'}, dimensions={0}, use_global_device_ids=true | all-gather | bytes 655360 | tf_op jit(solution)/shard_map/all_gather | solution.py:60
  95.0 21.3 %while.21 = (s32[]{:T(128)}, f32[8,128,256]{2,1,0:T(8,128)S(1)}, s32[8,8]{1,0:T(8,128)S(1)}, bf16[8,8,128,128]{3,2,1,0:T(8,128)(2,1)}, bf16[8,128,256]{2,1,0:T(8,128)(2,1)S(1)}, /*index=5*/s32[]{:T(128)}) while((s32[]{:T(128)}, f32[8,128,256]{2,1,0:T(8,128)S(1)}, s32[8,8]{1,0:T(8,128)S(1)}, bf16[8,8,128,128]{3,2,1,0:T(8,128)(2,1)}, ...), condition=%wide.region_6.7_spmd, body=%wide.region_4.6_spmd.sunk | while | flops 67371032 | bytes 4523185 | solution.py:72
  95.0 1.3 fusion.32
  96.3 1.3 scatter_fusion
  97.7 1.3 fusion.32
  99.0 1.3 scatter_fusion
  100.4 1.3 fusion.32
  101.6 1.3 scatter_fusion
  103.0 1.3 fusion.32
  104.3 1.3 scatter_fusion
  105.7 1.3 fusion.32
  107.0 1.3 scatter_fusion
  108.3 1.3 fusion.32
  109.6 1.3 scatter_fusion
  111.0 1.3 fusion.32
  112.3 1.3 scatter_fusion
  113.7 1.3 fusion.32
  114.9 1.3 scatter_fusion
  117.2 96.5 %all-reduce.2.cloned.1.call-done = f32[256,256]{1,0:T(8,128)} async-done(((f32[256,256]{1,0:T(8,128)}), f32[256,256]{1,0:T(8,128)}) %all-reduce.2.cloned.1.call-update) | async-done | bytes 262160 | tf_op jit(solution)/shard_map/psum | solution.py:63
  213.6 1.7 broadcast_multiply_fusion
  215.3 30.7 %reduce-scatter.5.cloned.1.call-done = bf16[128,256]{1,0:T(8,128)(2,1)} async-done(((bf16[1024,256]{1,0:T(8,128)(2,1)}), bf16[128,256]{1,0:T(8,128)(2,1)}) %reduce-scatter.5.cloned.1.call-update) | async-done | bytes 65552 | tf_op jit(solution)/shard_map/reduce_scatter | solution.py:74
  246.0 1.6 multiply_convert_fusion.3
  (66 shorter events, 23.2 us)
Async XLA Ops:
  7.2 74.5 %copy-start = (bf16[256,256]{1,0:T(8,128)(2,1)S(1)}, bf16[256,256]{1,0:T(8,128)(2,1)}, u32[]{:S(2)}) copy-start(bf16[256,256]{1,0:T(8,128)(2,1)} %param.16) | copy-start | bytes 393220
  7.2 25.1 %copy-start.3 = (bf16[128,256]{1,0:T(8,128)(2,1)S(1)}, bf16[128,256]{1,0:T(8,128)(2,1)}, u32[]{:S(2)}) copy-start(bf16[128,256]{1,0:T(8,128)(2,1)} %param.13) | copy-start | bytes 196612
  7.2 25.1 %copy-start.5 = (f32[128]{0:T(128)S(1)}, f32[128]{0:T(128)}, u32[]{:S(2)}) copy-start(f32[128]{0:T(128)} %param.14) | copy-start | bytes 1540
  7.2 41.7 %copy-start.4 = (s32[8,1,8]{2,1,0:T(1,128)S(1)}, s32[8,1,8]{2,1,0:T(1,128)}, u32[]{:S(2)}) copy-start(s32[8,1,8]{2,1,0:T(1,128)} %param.18) | copy-start | bytes 772
  7.2 74.5 %reduce-scatter.3.cloned.1.call-start = ((), (), s32[]{:S(2)}) async-start(), calls=%async_computation.2 | async-start | bytes 655360 | tf_op jit(solution)/shard_map/reduce_scatter | solution.py:49
  32.3 19.5 %copy-start.1 = (bf16[8,8,128,128]{3,2,1,0:T(8,128)(2,1)}, bf16[8,8,128,128]{3,2,1,0:T(8,128)(2,1)S(1)}, u32[]{:S(2)}) copy-start(bf16[8,8,128,128]{3,2,1,0:T(8,128)(2,1)S(1)} %get-tuple-element.175) | copy-start | bytes 6291460
  51.8 29.9 %copy-start.6 = (bf16[256,256]{1,0:T(8,128)(2,1)S(1)}, bf16[256,256]{1,0:T(8,128)(2,1)}, u32[]{:S(2)}) copy-start(bf16[256,256]{1,0:T(8,128)(2,1)} %param.17) | copy-start | bytes 393220
  55.7 157.9 %all-reduce.2.cloned.1.call-start = ((), (), s32[]{:S(2)}) async-start(), calls=%async_computation.3 | async-start | bytes 524288 | tf_op jit(solution)/shard_map/psum | solution.py:63
  81.7 2.2 copy-start.2
  84.9 161.1 %reduce-scatter.5.cloned.1.call-start = ((), (), s32[]{:S(2)}) async-start(), calls=%async_computation.4 | async-start | bytes 589824 | tf_op jit(solution)/shard_map/reduce_scatter | solution.py:74
Sparse Core Ops, SparseCore 0:
  55.8 25.8 reduce-scatter.2
  88.7 124.9 all-reduce.1
  216.0 29.9 reduce-scatter.4
where the time goes:
time: 255 us; the launch traced here: 254 us
  waiting for transfers between devices  152 us (60%)
  blocking collectives  26.5 us (10%)
  matrix products  21.2 us (8%)
  other arithmetic  20.2 us (8%)
  local copies, waits for them, and re-layouts  19.3 us (8%)
  between operations  13.9 us (5%)
    psum x1, waiting for transfers between devices, on_device(): weight_grad = lax.psum(local_grad, ('row', 'col')) / math.sqrt(total_nodes)  96.5 us
    reduce_scatter x1, waiting for transfers between devices, on_device(): lax.psum_scatter(rounded_terms, 'row', scatter_dimension=0, tiled=True)  30.7 us
    reduce_scatter x1, waiting for transfers between devices, on_device(): lax.psum_scatter(partial_value.astype(jnp.bfloat16), 'col', scatter_dimen...  25.2 us
    all_gather x1, blocking collectives, on_device(): lax.all_gather(scaled, 'row', axis=0, tiled=True).reshape(-1, B, width)  16.6 us
    scatter-add x8, other arithmetic, back_step(): return (carry.at[slot_now].add(contrib), None)  10.7 us
    dot_general x8, matrix products, back_step(): jnp.einsum('jab,af->jbf', tile_now, grad_now, preferred_element_type=jnp....  10.2 us
    all_gather x1, blocking collectives, on_device(): grad_y = lax.all_gather(grad_y_share, 'col', axis=0, tiled=True)  9.96 us
    dynamic_slice x8, local copies, waits for them, and re-layouts, on_device(): tiles = lax.map(densify, (edge_tgt[:, 0], edge_src[:, 0], tile_count[:, 0]))  9.94 us
  transfers between devices with their start and end apart: 3, of which 3 were waited for; matrix products, arithmetic and copies ran while one was open for 10% of the time, Pallas kernels for 0%

commit v1 on v0

v1 whole, which is shorter than its diff:
```python
import functools
import math

import jax
import jax.numpy as jnp
from jax import lax
from jax.experimental import pallas as pl
from jax.experimental.pallas import tpu as pltpu
from jax.sharding import PartitionSpec as P

B = 128
BF = jnp.bfloat16
F32 = jnp.float32
NN = (((1,), (0,)), ((), ()))
NT = (((1,), (1,)), ((), ()))
TN = (((0,), (0,)), ((), ()))


def dot(left, right, dims=NN):
    return lax.dot_general(left, right, dims, preferred_element_type=F32)


def each(first, last, body):
    if last - first <= 8:
        for index in range(first, last):
            body(index)
    else:
        lax.fori_loop(first, last, lambda index, carry: (body(index), carry)[1], 0)


def rows_at(index, size):
    return pl.ds(pl.multiple_of(index * size, size), size)


def to_column(row_of, parts, offset, rows):
    place = lax.broadcasted_iota(jnp.int32, (rows, B), 0) + offset
    lane = lax.broadcasted_iota(jnp.int32, (rows, B), 1)
    picked = jnp.zeros((rows, B), F32)
    for part in range(parts):
        picked = picked + jnp.where(lane + part * B == place, row_of(part), 0.0)
    return jnp.sum(picked, axis=1, keepdims=True)


def kernel(
    n_row,
    n_col,
    total_nodes,
    feat_ref,
    sscale_ref,
    tscale_ref,
    weight_ref,
    cot_ref,
    slot_ref,
    count_ref,
    tgt_ref,
    src_ref,
    act_ref,
    wgrad_ref,
    fgrad_ref,
    gath,
    adj,
    adj_t,
    edges,
    part_send,
    part_recv,
    gy,
    f_send,
    f_recv,
    w_send,
    w_recv,
    x_send,
    x_recv,
    w_all,
    g_ss,
    g_rs,
    p_ss,
    p_rs,
    y_ss,
    y_rs,
    f_ss,
    f_rs,
    w_ss,
    w_rs,
    x_ss,
    x_rs,
    o_ss,
    o_rs,
):
    row = lax.axis_index("row")
    col = lax.axis_index("col")
    own, width = feat_ref.shape
    share = cot_ref.shape[0]
    blocks, slots, entries = tgt_ref.shape
    per_block = slots * entries
    src_blocks = n_row * own // B
    chunk = weight_ref.shape[0] // n_row

    def row_peer(step):
        return lax.rem(row + step, n_row)

    def col_peer(step):
        return lax.rem(col + step, n_col)

    barrier = pltpu.get_barrier_semaphore()

    def greet_row(step):
        pl.semaphore_signal(
            barrier, 1, device_id=(row_peer(step), col), device_id_type=pl.DeviceIdType.MESH
        )

    def greet_col(step):
        pl.semaphore_signal(
            barrier, 1, device_id=(row, col_peer(step)), device_id_type=pl.DeviceIdType.MESH
        )

    each(1, n_row, greet_row)
    each(1, n_col, greet_col)

    def row_copy(source, target, send_sem, recv_sem, peer, at):
        return pltpu.make_async_remote_copy(
            src_ref=source,
            dst_ref=target.at[at],
            send_sem=send_sem.at[peer],
            recv_sem=recv_sem.at[at],
            device_id=(peer, col),
            device_id_type=pl.DeviceIdType.MESH,
        )

    def col_copy(source, target, send_sem, recv_sem, peer, at):
        return pltpu.make_async_remote_copy(
            src_ref=source,
            dst_ref=target.at[at],
            send_sem=send_sem.at[peer],
            recv_sem=recv_sem.at[at],
            device_id=(row, peer),
            device_id_type=pl.DeviceIdType.MESH,
        )

    source_col = to_column(lambda part: sscale_ref[pl.ds(part, 1), :], own // B, 0, own)
    gath[row] = (source_col * feat_ref[...].astype(F32)).astype(BF)
    pl.semaphore_wait(barrier, n_row + n_col - 2)

    def send_feat(step):
        row_copy(gath.at[row], gath, g_ss, g_rs, row_peer(step), row).start()

    each(1, n_row, send_feat)

    lane = lax.broadcasted_iota(jnp.int32, (entries, per_block), 1)
    spread = (lane % entries == lax.broadcasted_iota(jnp.int32, (entries, per_block), 0)).astype(
        F32
    ).astype(BF)
    slot_lane = lax.broadcasted_iota(jnp.int32, (slots, per_block), 1) // entries
    slot_hot = slot_lane == lax.broadcasted_iota(jnp.int32, (slots, per_block), 0)

    def flatten(ref):
        flat = ref[...].reshape(blocks * slots, entries).astype(F32).astype(BF)
        wide = dot(flat, spread).reshape(blocks, slots, per_block)
        return jnp.sum(jnp.where(slot_hot[None], wide, 0.0), axis=1)

    block_lane = lax.broadcasted_iota(jnp.int32, (blocks, per_block), 1) // entries
    alive = block_lane < count_ref[...]
    edges[0] = jnp.where(alive, flatten(tgt_ref), -1.0)
    edges[1] = flatten(src_ref)
    edges[2] = dot(slot_ref[...].astype(F32).astype(BF), slot_hot.astype(F32).astype(BF))

    place = lax.broadcasted_iota(jnp.int32, (B, per_block), 0).astype(F32)

    def fill(block, carry):
        target_hot = (place == edges[0, pl.ds(block, 1), :]).astype(F32).astype(BF)
        source_hot = (place == edges[1, pl.ds(block, 1), :]).astype(F32).astype(BF)
        slot_row = edges[2, pl.ds(block, 1), :]
        step = min(8, src_blocks)
        for begin in range(0, src_blocks, step):
            parts = []
            for source in range(begin, begin + step):
                here = (slot_row == float(source)).astype(F32).astype(BF)
                parts.append(source_hot * here)
            placed = jnp.concatenate(parts, axis=0)
            span = pl.ds(begin * B, step * B)
            adj[rows_at(block, B), span] = dot(target_hot, placed, NT).astype(BF)
            adj_t[span, rows_at(block, B)] = dot(placed, target_hot, NT).astype(BF)
        return carry

    lax.fori_loop(0, blocks, fill, 0)

    offset = col * share
    scale_share = to_column(
        lambda part: tscale_ref[pl.ds(part, 1), :], blocks, offset, share
    )

    def wait_feat(step):
        peer = row_peer(step)
        row_copy(gath.at[row], gath, g_ss, g_rs, peer, peer).wait()

    each(1, n_row, wait_feat)
    gathered = gath[...].reshape(n_row * own, width)

    def send_part(step):
        peer = col_peer(step)
        part_send[peer] = dot(adj[rows_at(peer, share), :], gathered).astype(BF)
        col_copy(part_send.at[peer], part_recv, p_ss, p_rs, peer, col).start()

    each(1, n_col, send_part)
    part_recv[col] = dot(adj[rows_at(col, share), :], gathered).astype(BF)

    def wait_part(step):
        peer = col_peer(step)
        col_copy(part_send.at[peer], part_recv, p_ss, p_rs, peer, peer).wait()

    each(1, n_col, wait_part)
    summed = jnp.sum(part_recv[...].astype(F32), axis=0)
    agg = (scale_share * summed).astype(BF)
    z_value = dot(agg, weight_ref[...])
    sigma = jax.nn.sigmoid(z_value)
    deriv = sigma * (1.0 + z_value * (1.0 - sigma))
    grad = (cot_ref[...].astype(F32) * deriv).astype(BF)
    gy[col] = (scale_share * dot(grad, weight_ref[...], NT)).astype(BF)

    def send_gy(step):
        col_copy(gy.at[col], gy, y_ss, y_rs, col_peer(step), col).start()

    each(1, n_col, send_gy)
    w_send[...] = dot(agg, grad, TN).reshape(n_row, chunk, width).astype(w_send.dtype)

    def send_w(step):
        peer = row_peer(step)
        row_copy(w_send.at[peer], w_recv, w_ss, w_rs, peer, row).start()

    each(1, n_row, send_w)
    w_recv[row] = w_send[row]
    act_ref[...] = (z_value * sigma).astype(BF)

    def wait_gy(step):
        peer = col_peer(step)
        col_copy(gy.at[col], gy, y_ss, y_rs, peer, peer).wait()

    def wait_w(step):
        peer = row_peer(step)
        row_copy(w_send.at[peer], w_recv, w_ss, w_rs, peer, peer).wait()

    each(1, n_row, wait_w)
    x_recv[col] = jnp.sum(w_recv[...].astype(F32), axis=0).astype(x_recv.dtype)

    def send_x(step):
        col_copy(x_recv.at[col], x_recv, x_ss, x_rs, col_peer(step), col).start()

    each(1, n_col, send_x)
    each(1, n_col, wait_gy)
    grad_y = gy[...].reshape(n_col * share, width)

    def send_f(step):
        peer = row_peer(step)
        f_send[peer] = dot(adj_t[rows_at(peer, own), :], grad_y).astype(BF)
        row_copy(f_send.at[peer], f_recv, f_ss, f_rs, peer, row).start()

    each(1, n_row, send_f)
    f_recv[row] = dot(adj_t[rows_at(row, own), :], grad_y).astype(BF)

    def wait_x(step):
        peer = col_peer(step)
        col_copy(x_recv.at[col], x_recv, x_ss, x_rs, peer, peer).wait()

    each(1, n_col, wait_x)
    w_all[row] = (
        jnp.sum(x_recv[...].astype(F32), axis=0) * (1.0 / math.sqrt(total_nodes))
    ).astype(w_all.dtype)

    def send_o(step):
        row_copy(w_all.at[row], w_all, o_ss, o_rs, row_peer(step), row).start()

    each(1, n_row, send_o)

    def wait_f(step):
        peer = row_peer(step)
        row_copy(f_send.at[peer], f_recv, f_ss, f_rs, peer, peer).wait()

    each(1, n_row, wait_f)
    fgrad_ref[...] = (source_col * jnp.sum(f_recv[...].astype(F32), axis=0)).astype(BF)

    def wait_o(step):
        peer = row_peer(step)
        row_copy(w_all.at[row], w_all, o_ss, o_rs, peer, peer).wait()

    each(1, n_row, wait_o)
    wgrad_ref[...] = w_all[...].astype(F32).reshape(wgrad_ref.shape)


def on_device(
    features,
    source_scale,
    target_scale,
    weight,
    cotangent,
    tile_src,
    tile_count,
    edge_tgt,
    edge_src,
    n_row,
    n_col,
):
    own, width = features.shape
    share = cotangent.shape[0]
    blocks, _, slots, entries = edge_tgt.shape
    targets = blocks * B
    sources = own * n_row
    chunk = width // n_row
    wtype = BF if chunk % 16 == 0 else F32
    vmem = pl.BlockSpec(memory_space=pltpu.VMEM)
    dma = pltpu.SemaphoreType.DMA
    row_sem, col_sem = dma((n_row,)), dma((n_col,))
    return pl.pallas_call(
        functools.partial(kernel, n_row, n_col, targets * n_row),
        out_shape=(
            jax.ShapeDtypeStruct((share, width), BF),
            jax.ShapeDtypeStruct((width, width), F32),
            jax.ShapeDtypeStruct((own, width), BF),
        ),
        in_specs=[vmem] * 9,
        out_specs=(vmem,) * 3,
        scratch_shapes=[
            pltpu.VMEM((n_row, own, width), BF),
            pltpu.VMEM((targets, sources), BF),
            pltpu.VMEM((sources, targets), BF),
            pltpu.VMEM((3, blocks, slots * entries), F32),
            pltpu.VMEM((n_col, share, width), BF),
            pltpu.VMEM((n_col, share, width), BF),
            pltpu.VMEM((n_col, share, width), BF),
            pltpu.VMEM((n_row, own, width), BF),
            pltpu.VMEM((n_row, own, width), BF),
            pltpu.VMEM((n_row, chunk, width), wtype),
            pltpu.VMEM((n_row, chunk, width), wtype),
            pltpu.VMEM((n_col, chunk, width), wtype),
            pltpu.VMEM((n_col, chunk, width), wtype),
            pltpu.VMEM((n_row, chunk, width), wtype),
            row_sem,
            row_sem,
            col_sem,
            col_sem,
            col_sem,
            col_sem,
            row_sem,
            row_sem,
            row_sem,
            row_sem,
            col_sem,
            col_sem,
            row_sem,
            row_sem,
        ],
        compiler_params=pltpu.CompilerParams(
            collective_id=0, has_side_effects=True, vmem_limit_bytes=48 * 1024 * 1024
        ),
        cost_estimate=pl.CostEstimate(
            flops=4 * targets * sources * width,
            bytes_accessed=4 * sources * width,
            transcendentals=share * width,
        ),
    )(
        features,
        source_scale.reshape(own // B, B),
        target_scale.reshape(blocks, B),
        weight,
        cotangent,
        tile_src[:, 0],
        tile_count,
        edge_tgt[:, 0],
        edge_src[:, 0],
    )


def solution(mesh):
    in_specs = (
        P(("col", "row"), None),
        P(("col", "row")),
        P("row"),
        P(),
        P(("row", "col"), None),
        P("row", "col", None),
        P("row", "col"),
        P("row", "col", None, None),
        P("row", "col", None, None),
    )
    out_specs = (P(("row", "col"), None), P(), P(("col", "row"), None))
    body = functools.partial(on_device, n_row=mesh.shape["row"], n_col=mesh.shape["col"])
    return jax.shard_map(
        body, mesh=mesh, in_specs=in_specs, out_specs=out_specs, check_vma=False
    )
```

time: 255 us -> 57.5 us (0.23)
  waiting for transfers between devices: 152 us -> 0 us
  Pallas kernels: 0 us -> 49.6 us
  blocking collectives: 26.5 us -> 0 us
  matrix products: 21.2 us -> 0 us
  other arithmetic: 20.2 us -> 0 us
  between operations: 13.9 us -> 0.69 us
  local copies, waits for them, and re-layouts: 19.3 us -> 6.86 us
    psum x1 -> x0, waiting for transfers between devices: 96.5 us -> none  [on_device(): weight_grad = lax.psum(local_grad, ('row', 'col')) / math.sqrt(total_nodes)]
    reduce_scatter x2 -> x0, waiting for transfers between devices: 55.9 us -> none  [the longest x1 30.7 us: on_device(): lax.psum_scatter(rounded_terms, 'row', scatter_dimension=0, tiled=True)]
    pallas_call x0 -> x1, Pallas kernels: none -> 49.6 us  [on_device(): pl.pallas_call(functools.partial(kernel, n_row, n_col, targets * n_row),...]
    all_gather x2 -> x0, blocking collectives: 26.5 us -> none  [the longest x1 16.6 us: on_device(): lax.all_gather(scaled, 'row', axis=0, tiled=True).reshape(-1, B, width)]
    dot_general x20 -> x0, matrix products: 21.2 us -> none  [the longest x8 10.2 us: back_step(): jnp.einsum('jab,af->jbf', tile_now, grad_now, preferred_element_type=jnp....]
    scatter-add x8 -> x0, other arithmetic: 10.7 us -> none  [back_step(): return (carry.at[slot_now].add(contrib), None)]
    dynamic_slice x9 -> x0, local copies, waits for them, and re-layouts: 10.7 us -> none  [the longest x8 9.94 us: on_device(): tiles = lax.map(densify, (edge_tgt[:, 0], edge_src[:, 0], tile_count[:, 0]))]
    unnamed x14 -> x22, local copies, waits for them, and re-layouts: 0.03 us -> 6.86 us
  transfers between devices with their start and end apart: 3 -> 0, of which waited for: 3 -> 0; matrix products, arithmetic and copies ran while one was open for 10% -> 0% of each run, Pallas kernels for 0% -> 0%
where the time goes in v1:
time: 57.5 us; the launch traced here: 57.1 us
  Pallas kernels  49.6 us (86%)
  local copies, waits for them, and re-layouts  6.86 us (12%)
  between operations  0.69 us (1%)
    pallas_call x1, Pallas kernels, on_device(): pl.pallas_call(functools.partial(kernel, n_row, n_col, targets * n_row),...  49.6 us
    unnamed x22, local copies, waits for them, and re-layouts  6.86 us

profile of v1, /device:TPU:0, one launch (start us, length us, event | category | flops | bytes accessed | tf_op | source)
XLA Modules:
  0.0 57.1 jit_solution(5246408102537837715)
XLA Ops:
  0.6 0.0 copy-start.8
  0.6 0.0 copy-start.7
  0.7 0.0 copy-start.5
  0.7 0.0 copy-start.6
  0.7 0.6 %copy-done.8 = s32[8,1]{0,1:T(1,128)S(1)} copy-done((s32[8,1]{0,1:T(1,128)S(1)}, s32[8,1]{0,1:T(1,128)}, u32[]{:S(2)}) %copy-start.8) | copy-done | bytes 56
  1.3 0.1 copy.12.count_ref
  1.4 0.0 copy-done.7
  1.4 0.0 copy-done.5
  1.4 0.0 copy-done.6
  1.4 0.0 copy-start
  1.4 0.9 %copy-done = bf16[256,256]{1,0:T(8,128)(2,1)S(1)} copy-done((bf16[256,256]{1,0:T(8,128)(2,1)S(1)}, bf16[256,256]{1,0:T(8,128)(2,1)}, u32[]{:S(2)}) %copy-start) | copy-done | bytes 131096
  2.3 0.0 copy-start.1
  2.3 0.9 %copy-done.1 = bf16[256,256]{1,0:T(8,128)(2,1)S(1)} copy-done((bf16[256,256]{1,0:T(8,128)(2,1)S(1)}, bf16[256,256]{1,0:T(8,128)(2,1)}, u32[]{:S(2)}) %copy-start.1) | copy-done | bytes 131096
  3.2 0.0 copy-start.2
  3.2 0.8 %copy-done.2 = bf16[128,256]{1,0:T(8,128)(2,1)S(1)} copy-done((bf16[128,256]{1,0:T(8,128)(2,1)S(1)}, bf16[128,256]{1,0:T(8,128)(2,1)}, u32[]{:S(2)}) %copy-start.2) | copy-done | bytes 65560
  4.0 0.0 copy-start.3
  4.0 0.8 %copy-done.3 = s32[8,1,8,32]{3,2,1,0:T(8,128)S(1)} copy-done((s32[8,1,8,32]{3,2,1,0:T(8,128)S(1)}, s32[8,1,8,32]{3,2,1,0:T(8,128)}, u32[]{:S(2)}) %copy-start.3) | copy-done | bytes 8216
  4.8 0.0 copy-start.4
  4.8 0.8 %copy-done.4 = s32[8,1,8,32]{3,2,1,0:T(8,128)S(1)} copy-done((s32[8,1,8,32]{3,2,1,0:T(8,128)S(1)}, s32[8,1,8,32]{3,2,1,0:T(8,128)}, u32[]{:S(2)}) %copy-start.4) | copy-done | bytes 8216
  5.5 49.6 %shard_map.112 = (bf16[256,256]{1,0:T(8,128)(2,1)S(1)}, f32[256,256]{1,0:T(8,128)S(1)}, bf16[128,256]{1,0:T(8,128)(2,1)S(1)}) custom-call(bf16[128,256]{1,0:T(8,128)(2,1)S(1)} %copy-done.2, f32[1,128]{1,0:T(1,128)S(1)} %bitcast.9, f32[8,128]{1,0:T(8,128)S(1)} %bitcast.7, bf16[256,256]{1,0:T(8,128)(2,1)S(1)} %copy-done, bf16[256,256]{1,0:T(8,128)(2,1)S(1)} %copy-done.1, ...), custom_call_target="tpu_custom_call" | custom-call | flops 1073741824 | bytes 1048576 | tf_op jit(solution)/shard_map/pallas_call | solution.py:311
  55.1 0.7 %copy.16 = bf16[256,256]{1,0:T(8,128)(2,1)} copy(bf16[256,256]{1,0:T(8,128)(2,1)S(1)} %get-tuple-element.6) | data formatting | bytes 262144
  55.8 0.7 %copy.17 = f32[256,256]{1,0:T(8,128)} copy(f32[256,256]{1,0:T(8,128)S(1)} %get-tuple-element.7) | data formatting | bytes 524288
  56.5 0.6 %copy.18 = bf16[128,256]{1,0:T(8,128)(2,1)} copy(bf16[128,256]{1,0:T(8,128)(2,1)S(1)} %get-tuple-element.8) | data formatting | bytes 131072
Async XLA Ops:
  0.6 0.7 %copy-start.8 = (s32[8,1]{0,1:T(1,128)S(1)}, s32[8,1]{0,1:T(1,128)}, u32[]{:S(2)}) copy-start(s32[8,1]{0,1:T(1,128)} %param.15) | copy-start | bytes 100
  0.6 0.7 %copy-start.7 = (f32[128]{0:T(128)S(1)}, f32[128]{0:T(128)}, u32[]{:S(2)}) copy-start(f32[128]{0:T(128)} %param.10) | copy-start | bytes 1540
  0.7 0.7 %copy-start.5 = (f32[1024]{0:T(1024)S(1)}, f32[1024]{0:T(1024)}, u32[]{:S(2)}) copy-start(f32[1024]{0:T(1024)} %param.11) | copy-start | bytes 12292
  0.7 0.7 %copy-start.6 = (s32[8,1,8]{2,1,0:T(1,128)S(1)}, s32[8,1,8]{2,1,0:T(1,128)}, u32[]{:S(2)}) copy-start(s32[8,1,8]{2,1,0:T(1,128)} %param.14) | copy-start | bytes 772
  1.4 0.9 %copy-start = (bf16[256,256]{1,0:T(8,128)(2,1)S(1)}, bf16[256,256]{1,0:T(8,128)(2,1)}, u32[]{:S(2)}) copy-start(bf16[256,256]{1,0:T(8,128)(2,1)} %weight_ref.1) | copy-start | bytes 393220
  2.3 0.9 %copy-start.1 = (bf16[256,256]{1,0:T(8,128)(2,1)S(1)}, bf16[256,256]{1,0:T(8,128)(2,1)}, u32[]{:S(2)}) copy-start(bf16[256,256]{1,0:T(8,128)(2,1)} %cot_ref.1) | copy-start | bytes 393220
  3.2 0.8 %copy-start.2 = (bf16[128,256]{1,0:T(8,128)(2,1)S(1)}, bf16[128,256]{1,0:T(8,128)(2,1)}, u32[]{:S(2)}) copy-start(bf16[128,256]{1,0:T(8,128)(2,1)} %feat_ref.1) | copy-start | bytes 196612
  4.0 0.8 %copy-start.3 = (s32[8,1,8,32]{3,2,1,0:T(8,128)S(1)}, s32[8,1,8,32]{3,2,1,0:T(8,128)}, u32[]{:S(2)}) copy-start(s32[8,1,8,32]{3,2,1,0:T(8,128)} %param.16) | copy-start | bytes 24580
  4.8 0.8 %copy-start.4 = (s32[8,1,8,32]{3,2,1,0:T(8,128)S(1)}, s32[8,1,8,32]{3,2,1,0:T(8,128)}, u32[]{:S(2)}) copy-start(s32[8,1,8,32]{3,2,1,0:T(8,128)} %param.17) | copy-start | bytes 24580

commit v2 on v1

v2 whole, which is shorter than its diff:
```python
import functools
import math

import jax
import jax.numpy as jnp
from jax import lax
from jax.experimental import pallas as pl
from jax.experimental.pallas import tpu as pltpu
from jax.sharding import PartitionSpec as P

B = 128
BF = jnp.bfloat16
F32 = jnp.float32
NN = (((1,), (0,)), ((), ()))
NT = (((1,), (1,)), ((), ()))
TN = (((0,), (0,)), ((), ()))


def dot(left, right, dims=NN):
    return lax.dot_general(left, right, dims, preferred_element_type=F32)


def each(first, last, body):
    if last - first <= 8:
        for index in range(first, last):
            body(index)
    else:
        lax.fori_loop(first, last, lambda index, carry: (body(index), carry)[1], 0)


def rows_at(index, size):
    return pl.ds(pl.multiple_of(index * size, size), size)


def to_column(row_of, parts, offset, rows):
    place = lax.broadcasted_iota(jnp.int32, (rows, B), 0) + offset
    lane = lax.broadcasted_iota(jnp.int32, (rows, B), 1)
    picked = jnp.zeros((rows, B), F32)
    for part in range(parts):
        picked = picked + jnp.where(lane + part * B == place, row_of(part), 0.0)
    return jnp.sum(picked, axis=1, keepdims=True)


def kernel(
    n_row,
    n_col,
    total_nodes,
    feat_hbm,
    sscale_hbm,
    tscale_hbm,
    weight_hbm,
    cot_hbm,
    slot_hbm,
    count_hbm,
    tgt_hbm,
    src_hbm,
    act_ref,
    wgrad_ref,
    fgrad_ref,
    feat_ref,
    sscale_ref,
    tscale_ref,
    weight_ref,
    cot_ref,
    slot_ref,
    count_ref,
    tgt_ref,
    src_ref,
    gath,
    adj,
    adj_t,
    edges,
    part_send,
    part_recv,
    agg,
    gy,
    f_pair,
    f_got,
    f_send,
    f_recv,
    w_pair,
    w_got,
    w_send,
    w_recv,
    x_all,
    w_all,
    in_sem,
    g_ss,
    g_rs,
    gp_ss,
    gp_rs,
    p_ss,
    p_rs,
    y_ss,
    y_rs,
    fp_ss,
    fp_rs,
    f_ss,
    f_rs,
    wp_ss,
    wp_rs,
    w_ss,
    w_rs,
    x_ss,
    x_rs,
    o_ss,
    o_rs,
    op_ss,
    op_rs,
):
    row = lax.axis_index("row")
    col = lax.axis_index("col")
    core = lax.rem(row, 2)
    level = lax.div(row, 2)
    n_z = n_row // 2
    own, width = feat_ref.shape
    half = width // 2
    share = cot_ref.shape[0]
    blocks, slots, entries = tgt_ref.shape
    per_block = slots * entries
    chunk = half // n_z
    other_row = row + 1 - 2 * core

    loads = [
        pltpu.make_async_copy(source, target, in_sem.at[index])
        for index, (source, target) in enumerate(
            (
                (feat_hbm, feat_ref),
                (sscale_hbm, sscale_ref),
                (count_hbm, count_ref),
                (slot_hbm, slot_ref),
                (tgt_hbm, tgt_ref),
                (src_hbm, src_ref),
                (tscale_hbm, tscale_ref),
                (weight_hbm, weight_ref),
                (cot_hbm, cot_ref),
            )
        )
    ]
    barrier = pltpu.get_barrier_semaphore()

    def line_peer(step):
        return lax.rem(level + step, n_z)

    def col_peer(step):
        return lax.rem(col + step, n_col)

    def greet(peer_row, peer_col):
        pl.semaphore_signal(
            barrier, 1, device_id=(peer_row, peer_col), device_id_type=pl.DeviceIdType.MESH
        )

    greet(other_row, col)
    each(1, n_z, lambda step: greet(line_peer(step) * 2 + core, col))
    each(1, n_col, lambda step: greet(row, col_peer(step)))
    for load in loads:
        load.start()

    def remote(source, target, send_sem, recv_sem, peer_row, peer_col):
        return pltpu.make_async_remote_copy(
            src_ref=source,
            dst_ref=target,
            send_sem=send_sem,
            recv_sem=recv_sem,
            device_id=(peer_row, peer_col),
            device_id_type=pl.DeviceIdType.MESH,
        )

    def on_line(source, target, send_sem, recv_sem, peer, at):
        return remote(
            source, target(at), send_sem.at[peer], recv_sem.at[at], peer * 2 + core, col
        )

    def on_col(source, target, send_sem, recv_sem, peer, at):
        return remote(source, target.at[at], send_sem.at[peer], recv_sem.at[at], row, peer)

    loads[0].wait()
    loads[1].wait()
    source_col = to_column(lambda part: sscale_ref[pl.ds(part, 1), :], own // B, 0, own)
    scaled = (source_col * feat_ref[...].astype(F32)).astype(BF)
    for part in range(2):
        gath[part, core, level] = scaled[:, part * half : (part + 1) * half]
    pl.semaphore_wait(barrier, n_z + n_col - 1)

    def feat_copy(part, peer, at):
        return on_line(
            gath.at[part, core, level],
            lambda place: gath.at[part, core, place],
            g_ss.at[part],
            g_rs.at[part],
            peer,
            at,
        )

    def feat_pair(part, of_core):
        line = gath.at[part, of_core]
        return remote(line, line, gp_ss.at[part], gp_rs.at[part], other_row, col)

    def send_feat(part):
        each(1, n_z, lambda step: feat_copy(part, line_peer(step), level).start())

    def forward_feat(part):
        def wait(step):
            feat_copy(part, line_peer(step), line_peer(step)).wait()

        each(1, n_z, wait)
        feat_pair(part, core).start()

    send_feat(0)
    for load in loads[2:7]:
        load.wait()

    lane = lax.broadcasted_iota(jnp.int32, (entries, per_block), 1)
    spread = (lane % entries == lax.broadcasted_iota(jnp.int32, (entries, per_block), 0)).astype(
        F32
    ).astype(BF)
    slot_lane = lax.broadcasted_iota(jnp.int32, (slots, per_block), 1) // entries
    slot_hot = slot_lane == lax.broadcasted_iota(jnp.int32, (slots, per_block), 0)

    def flatten(ref):
        flat = ref[...].reshape(blocks * slots, entries).astype(F32).astype(BF)
        wide = dot(flat, spread).reshape(blocks, slots, per_block)
        return jnp.sum(jnp.where(slot_hot[None], wide, 0.0), axis=1)

    block_lane = lax.broadcasted_iota(jnp.int32, (blocks, per_block), 1) // entries
    square = (blocks, blocks)
    diagonal = lax.broadcasted_iota(jnp.int32, square, 0) == lax.broadcasted_iota(
        jnp.int32, square, 1
    )
    counts = jnp.sum(
        jnp.where(diagonal, count_ref[...].astype(F32), 0.0), axis=1, keepdims=True
    )
    alive = block_lane.astype(F32) < counts
    edges[0] = jnp.where(alive, flatten(tgt_ref), -1.0)
    edges[1] = flatten(src_ref)
    edges[2] = dot(slot_ref[...].astype(F32).astype(BF), slot_hot.astype(F32).astype(BF))

    place = lax.broadcasted_iota(jnp.int32, (B, per_block), 0).astype(F32)

    def fill(block, carry):
        target_hot = (place == edges[0, pl.ds(block, 1), :]).astype(F32).astype(BF)
        source_hot = (place == edges[1, pl.ds(block, 1), :]).astype(F32).astype(BF)
        slot_row = edges[2, pl.ds(block, 1), :]
        step = min(8, n_row)
        for begin in range(0, n_row, step):
            parts = []
            for at in range(begin, begin + step):
                source = (at % n_z) * 2 + at // n_z
                here = (slot_row == float(source)).astype(F32).astype(BF)
                parts.append(source_hot * here)
            placed = jnp.concatenate(parts, axis=0)
            span = pl.ds(begin * B, step * B)
            adj[rows_at(block, B), span] = dot(target_hot, placed, NT).astype(BF)
            adj_t[span, rows_at(block, B)] = dot(placed, target_hot, NT).astype(BF)
        return carry

    lax.fori_loop(0, blocks // 2, fill, 0)
    send_feat(1)
    forward_feat(0)
    lax.fori_loop(blocks // 2, blocks, fill, 0)
    scale_share = to_column(
        lambda part: tscale_ref[pl.ds(part, 1), :], blocks, col * share, share
    )

    def part_copy(part, peer, at):
        return on_col(
            part_send.at[part, peer],
            part_recv.at[part],
            p_ss.at[part],
            p_rs.at[part],
            peer,
            at,
        )

    def forward(part):
        feat_pair(part, 1 - core).wait_recv()
        feat_pair(part, core).wait_send()
        gathered = gath[part].reshape(n_row * own, half)

        def send_part(step):
            peer = col_peer(step)
            part_send[part, peer] = dot(adj[rows_at(peer, share), :], gathered).astype(BF)
            part_copy(part, peer, col).start()

        each(1, n_col, send_part)
        part_recv[part, col] = dot(adj[rows_at(col, share), :], gathered).astype(BF)

    forward(0)
    forward_feat(1)
    forward(1)
    loads[7].wait()
    loads[8].wait()

    z_value = jnp.zeros((share, width), F32)
    for part in range(2):
        each(1, n_col, lambda step: part_copy(part, col_peer(step), col_peer(step)).wait())
        summed = jnp.sum(part_recv[part].astype(F32), axis=0)
        agg_part = (scale_share * summed).astype(BF)
        agg[part] = agg_part
        z_value = z_value + dot(agg_part, weight_ref[part * half : (part + 1) * half, :])
    sigma = jax.nn.sigmoid(z_value)
    deriv = sigma * (1.0 + z_value * (1.0 - sigma))
    grad = (cot_ref[...].astype(F32) * deriv).astype(BF)

    def gy_copy(part, peer, at):
        return on_col(
            gy.at[part, col], gy.at[part], y_ss.at[part], y_rs.at[part], peer, at
        )

    for part in range(2):
        rows = weight_ref[part * half : (part + 1) * half, :]
        gy[part, col] = (scale_share * dot(grad, rows, NT)).astype(BF)
        each(1, n_col, lambda step: gy_copy(part, col_peer(step), col).start())

    w_pair[...] = (
        dot(agg[1 - core], grad, TN).reshape(n_z, chunk, width).astype(w_pair.dtype)
    )
    pair_w = remote(w_pair, w_got, wp_ss, wp_rs, other_row, col)
    pair_w.start()
    act_ref[...] = (z_value * sigma).astype(BF)
    mine = dot(agg[core], grad, TN).reshape(n_z, chunk, width)

    def w_copy(peer, at):
        return on_line(
            w_send.at[peer], lambda place: w_recv.at[place], w_ss, w_rs, peer, at
        )

    pair_w.wait()
    w_send[...] = (mine + w_got[...].astype(F32)).astype(w_send.dtype)
    each(1, n_z, lambda step: w_copy(line_peer(step), level).start())
    w_recv[level] = w_send[level]

    def f_pair_copy(part):
        return remote(
            f_pair.at[part], f_got.at[part], fp_ss.at[part], fp_rs.at[part], other_row, col
        )

    def f_copy(part, peer, at):
        return on_line(
            f_send.at[part, peer],
            lambda place: f_recv.at[part, place],
            f_ss.at[part],
            f_rs.at[part],
            peer,
            at,
        )

    def x_copy(peer, at):
        return on_col(x_all.at[col], x_all, x_ss, x_rs, peer, at)

    def o_copy(peer, at):
        return on_line(
            w_all.at[core, level], lambda place: w_all.at[core, place], o_ss, o_rs, peer, at
        )

    for part in range(2):
        each(1, n_col, lambda step: gy_copy(part, col_peer(step), col_peer(step)).wait())
        grad_y = gy[part].reshape(n_col * share, half)
        line = n_z * own
        f_pair[part] = (
            dot(adj_t[rows_at(1 - core, line), :], grad_y).reshape(n_z, own, half).astype(BF)
        )
        f_pair_copy(part).start()
        kept = dot(adj_t[rows_at(core, line), :], grad_y).reshape(n_z, own, half)
        if part == 0:
            each(1, n_z, lambda step: w_copy(line_peer(step), line_peer(step)).wait())
            x_all[col] = jnp.sum(w_recv[...].astype(F32), axis=0).astype(x_all.dtype)
            each(1, n_col, lambda step: x_copy(col_peer(step), col).start())
        f_pair_copy(part).wait()
        f_send[part] = (kept + f_got[part].astype(F32)).astype(BF)
        each(1, n_z, lambda step: f_copy(part, line_peer(step), level).start())
        f_recv[part, level] = f_send[part, level]

    each(1, n_col, lambda step: x_copy(col_peer(step), col_peer(step)).wait())
    w_all[core, level] = (
        jnp.sum(x_all[...].astype(F32), axis=0) * (1.0 / math.sqrt(total_nodes))
    ).astype(w_all.dtype)
    each(1, n_z, lambda step: o_copy(line_peer(step), level).start())

    def pair_o(of_core):
        return remote(w_all.at[of_core], w_all.at[of_core], op_ss, op_rs, other_row, col)

    def finish(part):
        each(1, n_z, lambda step: f_copy(part, line_peer(step), line_peer(step)).wait())
        fgrad_ref[:, part * half : (part + 1) * half] = (
            source_col * jnp.sum(f_recv[part].astype(F32), axis=0)
        ).astype(BF)

    finish(0)
    each(1, n_z, lambda step: o_copy(line_peer(step), line_peer(step)).wait())
    pair_o(core).start()
    finish(1)
    pair_o(1 - core).wait_recv()
    pair_o(core).wait_send()
    wgrad_ref[...] = w_all[...].astype(F32).reshape(wgrad_ref.shape)


def on_device(
    features,
    source_scale,
    target_scale,
    weight,
    cotangent,
    tile_src,
    tile_count,
    edge_tgt,
    edge_src,
    n_row,
    n_col,
):
    own, width = features.shape
    share = cotangent.shape[0]
    blocks, _, slots, entries = edge_tgt.shape
    targets = blocks * B
    sources = own * n_row
    n_z = n_row // 2
    half = width // 2
    chunk = half // n_z
    wtype = BF if chunk % 16 == 0 else F32
    operands = (
        features,
        source_scale.reshape(own // B, B),
        target_scale.reshape(blocks, B),
        weight,
        cotangent,
        tile_src[:, 0],
        tile_count.reshape(1, blocks),
        edge_tgt[:, 0],
        edge_src[:, 0],
    )
    vmem = pl.BlockSpec(memory_space=pltpu.VMEM)
    dma = pltpu.SemaphoreType.DMA
    return pl.pallas_call(
        functools.partial(kernel, n_row, n_col, targets * n_row),
        out_shape=(
            jax.ShapeDtypeStruct((share, width), BF),
            jax.ShapeDtypeStruct((width, width), F32),
            jax.ShapeDtypeStruct((own, width), BF),
        ),
        in_specs=[pl.BlockSpec(memory_space=pltpu.HBM)] * 9,
        out_specs=(vmem,) * 3,
        scratch_shapes=[pltpu.VMEM(item.shape, item.dtype) for item in operands]
        + [
            pltpu.VMEM((2, 2, n_z, own, half), BF),
            pltpu.VMEM((targets, sources), BF),
            pltpu.VMEM((sources, targets), BF),
            pltpu.VMEM((3, blocks, slots * entries), F32),
            pltpu.VMEM((2, n_col, share, half), BF),
            pltpu.VMEM((2, n_col, share, half), BF),
            pltpu.VMEM((2, share, half), BF),
            pltpu.VMEM((2, n_col, share, half), BF),
        ]
        + [pltpu.VMEM((2, n_z, own, half), BF)] * 4
        + [pltpu.VMEM((n_z, chunk, width), wtype)] * 4
        + [
            pltpu.VMEM((n_col, chunk, width), wtype),
            pltpu.VMEM((2, n_z, chunk, width), wtype),
            dma((9,)),
        ]
        + [dma((2, n_z))] * 2
        + [dma((2,))] * 2
        + [dma((2, n_col))] * 4
        + [dma((2,))] * 2
        + [dma((2, n_z))] * 2
        + [dma(())] * 2
        + [dma((n_z,))] * 2
        + [dma((n_col,))] * 2
        + [dma((n_z,))] * 2
        + [dma(())] * 2,
        compiler_params=pltpu.CompilerParams(
            collective_id=0, has_side_effects=True, vmem_limit_bytes=48 * 1024 * 1024
        ),
        cost_estimate=pl.CostEstimate(
            flops=4 * targets * sources * width,
            bytes_accessed=4 * sources * width,
            transcendentals=share * width,
        ),
    )(*operands)


def solution(mesh):
    in_specs = (
        P(("col", "row"), None),
        P(("col", "row")),
        P("row"),
        P(),
        P(("row", "col"), None),
        P("row", "col", None),
        P("row", "col"),
        P("row", "col", None, None),
        P("row", "col", None, None),
    )
    out_specs = (P(("row", "col"), None), P(), P(("col", "row"), None))
    body = functools.partial(on_device, n_row=mesh.shape["row"], n_col=mesh.shape["col"])
    return jax.shard_map(
        body, mesh=mesh, in_specs=in_specs, out_specs=out_specs, check_vma=False
    )
```

time: 57.5 us -> 46.9 us (0.82)
  Pallas kernels: 49.6 us -> 39.1 us
    pallas_call x1, Pallas kernels: 49.6 us -> 39.1 us  [on_device(): pl.pallas_call(functools.partial(kernel, n_row, n_col, targets * n_row),...]
    unnamed x22 -> x21, local copies, waits for them, and re-layouts: 6.86 us -> 6.83 us
where the time goes in v2:
time: 46.9 us; the launch traced here: 46.6 us
  Pallas kernels  39.1 us (83%)
  local copies, waits for them, and re-layouts  6.83 us (15%)
  between operations  0.68 us (1%)
    pallas_call x1, Pallas kernels, on_device(): pl.pallas_call(functools.partial(kernel, n_row, n_col, targets * n_row),...  39.1 us
    unnamed x21, local copies, waits for them, and re-layouts  6.83 us

profile of v2, /device:TPU:0, one launch (start us, length us, event | category | flops | bytes accessed | tf_op | source)
XLA Modules:
  0.0 46.6 jit_solution(5669608840523290974)
XLA Ops:
  0.6 0.0 copy-start.6
  0.6 0.0 copy-start.5
  0.7 0.0 copy-start.7
  0.7 0.0 copy-start.8
  0.7 0.6 %copy-done.6 = s32[8,1,8]{2,1,0:T(1,128)S(1)} copy-done((s32[8,1,8]{2,1,0:T(1,128)S(1)}, s32[8,1,8]{2,1,0:T(1,128)}, u32[]{:S(2)}) %copy-start.6) | copy-done | bytes 280
  1.3 0.0 copy-done.5
  1.3 0.0 copy-done.7
  1.3 0.0 copy-done.8
  1.3 0.0 copy-start
  1.3 0.9 %copy-done = bf16[256,256]{1,0:T(8,128)(2,1)S(1)} copy-done((bf16[256,256]{1,0:T(8,128)(2,1)S(1)}, bf16[256,256]{1,0:T(8,128)(2,1)}, u32[]{:S(2)}) %copy-start) | copy-done | bytes 131096
  2.2 0.0 copy-start.1
  2.3 0.9 %copy-done.1 = bf16[256,256]{1,0:T(8,128)(2,1)S(1)} copy-done((bf16[256,256]{1,0:T(8,128)(2,1)S(1)}, bf16[256,256]{1,0:T(8,128)(2,1)}, u32[]{:S(2)}) %copy-start.1) | copy-done | bytes 131096
  3.2 0.0 copy-start.2
  3.2 0.8 %copy-done.2 = bf16[128,256]{1,0:T(8,128)(2,1)S(1)} copy-done((bf16[128,256]{1,0:T(8,128)(2,1)S(1)}, bf16[128,256]{1,0:T(8,128)(2,1)}, u32[]{:S(2)}) %copy-start.2) | copy-done | bytes 65560
  4.0 0.0 copy-start.3
  4.0 0.8 %copy-done.3 = s32[8,1,8,32]{3,2,1,0:T(8,128)S(1)} copy-done((s32[8,1,8,32]{3,2,1,0:T(8,128)S(1)}, s32[8,1,8,32]{3,2,1,0:T(8,128)}, u32[]{:S(2)}) %copy-start.3) | copy-done | bytes 8216
  4.8 0.0 copy-start.4
  4.8 0.8 %copy-done.4 = s32[8,1,8,32]{3,2,1,0:T(8,128)S(1)} copy-done((s32[8,1,8,32]{3,2,1,0:T(8,128)S(1)}, s32[8,1,8,32]{3,2,1,0:T(8,128)}, u32[]{:S(2)}) %copy-start.4) | copy-done | bytes 8216
  5.5 39.1 %shard_map.112 = (bf16[256,256]{1,0:T(8,128)(2,1)S(1)}, f32[256,256]{1,0:T(8,128)S(1)}, bf16[128,256]{1,0:T(8,128)(2,1)S(1)}) custom-call(bf16[128,256]{1,0:T(8,128)(2,1)S(1)} %copy-done.2, f32[1,128]{1,0:T(1,128)S(1)} %bitcast.10, f32[8,128]{1,0:T(8,128)S(1)} %bitcast.8, bf16[256,256]{1,0:T(8,128)(2,1)S(1)} %copy-done, bf16[256,256]{1,0:T(8,128)(2,1)S(1)} %copy-done.1, ...), custom_call_target="tpu_custom_call" | custom-call | flops 1073741824 | bytes 1048576 | tf_op jit(solution)/shard_map/pallas_call | solution.py:433
  44.6 0.7 %copy.15 = bf16[256,256]{1,0:T(8,128)(2,1)} copy(bf16[256,256]{1,0:T(8,128)(2,1)S(1)} %get-tuple-element.6) | data formatting | bytes 262144
  45.2 0.7 %copy.16 = f32[256,256]{1,0:T(8,128)} copy(f32[256,256]{1,0:T(8,128)S(1)} %get-tuple-element.7) | data formatting | bytes 524288
  45.9 0.6 %copy.17 = bf16[128,256]{1,0:T(8,128)(2,1)} copy(bf16[128,256]{1,0:T(8,128)(2,1)S(1)} %get-tuple-element.8) | data formatting | bytes 131072
Async XLA Ops:
  0.6 0.7 %copy-start.6 = (s32[8,1,8]{2,1,0:T(1,128)S(1)}, s32[8,1,8]{2,1,0:T(1,128)}, u32[]{:S(2)}) copy-start(s32[8,1,8]{2,1,0:T(1,128)} %param.14) | copy-start | bytes 772
  0.6 0.7 %copy-start.5 = (f32[1024]{0:T(1024)S(1)}, f32[1024]{0:T(1024)}, u32[]{:S(2)}) copy-start(f32[1024]{0:T(1024)} %param.11) | copy-start | bytes 12292
  0.7 0.7 %copy-start.7 = (f32[128]{0:T(128)S(1)}, f32[128]{0:T(128)}, u32[]{:S(2)}) copy-start(f32[128]{0:T(128)} %param.10) | copy-start | bytes 1540
  0.7 0.7 %copy-start.8 = (s32[8,1]{0,1:T(1,128)S(1)}, s32[8,1]{0,1:T(1,128)}, u32[]{:S(2)}) copy-start(s32[8,1]{0,1:T(1,128)} %param.15) | copy-start | bytes 100
  1.3 0.9 %copy-start = (bf16[256,256]{1,0:T(8,128)(2,1)S(1)}, bf16[256,256]{1,0:T(8,128)(2,1)}, u32[]{:S(2)}) copy-start(bf16[256,256]{1,0:T(8,128)(2,1)} %weight_hbm.1) | copy-start | bytes 393220
  2.2 0.9 %copy-start.1 = (bf16[256,256]{1,0:T(8,128)(2,1)S(1)}, bf16[256,256]{1,0:T(8,128)(2,1)}, u32[]{:S(2)}) copy-start(bf16[256,256]{1,0:T(8,128)(2,1)} %cot_hbm.1) | copy-start | bytes 393220
  3.2 0.8 %copy-start.2 = (bf16[128,256]{1,0:T(8,128)(2,1)S(1)}, bf16[128,256]{1,0:T(8,128)(2,1)}, u32[]{:S(2)}) copy-start(bf16[128,256]{1,0:T(8,128)(2,1)} %feat_hbm.1) | copy-start | bytes 196612
  4.0 0.8 %copy-start.3 = (s32[8,1,8,32]{3,2,1,0:T(8,128)S(1)}, s32[8,1,8,32]{3,2,1,0:T(8,128)}, u32[]{:S(2)}) copy-start(s32[8,1,8,32]{3,2,1,0:T(8,128)} %param.16) | copy-start | bytes 24580
  4.8 0.8 %copy-start.4 = (s32[8,1,8,32]{3,2,1,0:T(8,128)S(1)}, s32[8,1,8,32]{3,2,1,0:T(8,128)}, u32[]{:S(2)}) copy-start(s32[8,1,8,32]{3,2,1,0:T(8,128)} %param.17) | copy-start | bytes 24580

commit v3 on v2

--- a/solution.py
+++ b/solution.py
@@ -54,6 +54,9 @@
     count_hbm,
     tgt_hbm,
     src_hbm,
+    act_hbm,
+    wgrad_hbm,
+    fgrad_hbm,
     act_ref,
     wgrad_ref,
     fgrad_ref,
@@ -85,6 +88,7 @@
     x_all,
     w_all,
     in_sem,
+    out_sem,
     g_ss,
     g_rs,
     gp_ss,
@@ -137,6 +141,12 @@
             )
         )
     ]
+    stores = [
+        pltpu.make_async_copy(source, target, out_sem.at[index])
+        for index, (source, target) in enumerate(
+            ((act_ref, act_hbm), (fgrad_ref, fgrad_hbm), (wgrad_ref, wgrad_hbm))
+        )
+    ]
     barrier = pltpu.get_barrier_semaphore()
 
     def line_peer(step):
@@ -318,6 +328,7 @@
     pair_w = remote(w_pair, w_got, wp_ss, wp_rs, other_row, col)
     pair_w.start()
     act_ref[...] = (z_value * sigma).astype(BF)
+    stores[0].start()
     mine = dot(agg[core], grad, TN).reshape(n_z, chunk, width)
 
     def w_copy(peer, at):
@@ -353,6 +364,10 @@
             w_all.at[core, level], lambda place: w_all.at[core, place], o_ss, o_rs, peer, at
         )
 
+    each(1, n_z, lambda step: w_copy(line_peer(step), line_peer(step)).wait())
+    x_all[col] = jnp.sum(w_recv[...].astype(F32), axis=0).astype(x_all.dtype)
+    each(1, n_col, lambda step: x_copy(col_peer(step), col).start())
+
     for part in range(2):
         each(1, n_col, lambda step: gy_copy(part, col_peer(step), col_peer(step)).wait())
         grad_y = gy[part].reshape(n_col * share, half)
@@ -362,20 +377,16 @@
         )
         f_pair_copy(part).start()
         kept = dot(adj_t[rows_at(core, line), :], grad_y).reshape(n_z, own, half)
-        if part == 0:
-            each(1, n_z, lambda step: w_copy(line_peer(step), line_peer(step)).wait())
-            x_all[col] = jnp.sum(w_recv[...].astype(F32), axis=0).astype(x_all.dtype)
-            each(1, n_col, lambda step: x_copy(col_peer(step), col).start())
+        if part == 1:
+            each(1, n_col, lambda step: x_copy(col_peer(step), col_peer(step)).wait())
+            w_all[core, level] = (
+                jnp.sum(x_all[...].astype(F32), axis=0) * (1.0 / math.sqrt(total_nodes))
+            ).astype(w_all.dtype)
+            each(1, n_z, lambda step: o_copy(line_peer(step), level).start())
         f_pair_copy(part).wait()
         f_send[part] = (kept + f_got[part].astype(F32)).astype(BF)
         each(1, n_z, lambda step: f_copy(part, line_peer(step), level).start())
         f_recv[part, level] = f_send[part, level]
-
-    each(1, n_col, lambda step: x_copy(col_peer(step), col_peer(step)).wait())
-    w_all[core, level] = (
-        jnp.sum(x_all[...].astype(F32), axis=0) * (1.0 / math.sqrt(total_nodes))
-    ).astype(w_all.dtype)
-    each(1, n_z, lambda step: o_copy(line_peer(step), level).start())
 
     def pair_o(of_core):
         return remote(w_all.at[of_core], w_all.at[of_core], op_ss, op_rs, other_row, col)
@@ -390,9 +401,32 @@
     each(1, n_z, lambda step: o_copy(line_peer(step), line_peer(step)).wait())
     pair_o(core).start()
     finish(1)
+    stores[1].start()
     pair_o(1 - core).wait_recv()
     pair_o(core).wait_send()
     wgrad_ref[...] = w_all[...].astype(F32).reshape(wgrad_ref.shape)
+    stores[2].start()
+    for store in stores:
+        store.wait()
+
+
+def hand_on(*refs):
+    load_sem, store_sem = refs[9:]
+    loads = [
+        pltpu.make_async_copy(refs[index], refs[6 + index], load_sem.at[index])
+        for index in range(3)
+    ]
+    stores = [
+        pltpu.make_async_copy(refs[6 + index], refs[3 + index], store_sem.at[index])
+        for index in range(3)
+    ]
+    for load in loads:
+        load.start()
+    for load, store in zip(loads, stores):
+        load.wait()
+        store.start()
+    for store in stores:
+        store.wait()
 
 
 def on_device(
@@ -428,18 +462,19 @@
         edge_tgt[:, 0],
         edge_src[:, 0],
     )
-    vmem = pl.BlockSpec(memory_space=pltpu.VMEM)
     dma = pltpu.SemaphoreType.DMA
-    return pl.pallas_call(
+    shapes = (
+        jax.ShapeDtypeStruct((share, width), BF),
+        jax.ShapeDtypeStruct((width, width), F32),
+        jax.ShapeDtypeStruct((own, width), BF),
+    )
+    hbm = pl.BlockSpec(memory_space=pltpu.HBM)
+    results = pl.pallas_call(
         functools.partial(kernel, n_row, n_col, targets * n_row),
-        out_shape=(
-            jax.ShapeDtypeStruct((share, width), BF),
-            jax.ShapeDtypeStruct((width, width), F32),
-            jax.ShapeDtypeStruct((own, width), BF),
-        ),
-        in_specs=[pl.BlockSpec(memory_space=pltpu.HBM)] * 9,
-        out_specs=(vmem,) * 3,
-        scratch_shapes=[pltpu.VMEM(item.shape, item.dtype) for item in operands]
+        out_shape=shapes,
+        in_specs=[hbm] * 9,
+        out_specs=(hbm,) * 3,
+        scratch_shapes=[pltpu.VMEM(item.shape, item.dtype) for item in shapes + operands]
         + [
             pltpu.VMEM((2, 2, n_z, own, half), BF),
             pltpu.VMEM((targets, sources), BF),
@@ -456,6 +491,7 @@
             pltpu.VMEM((n_col, chunk, width), wtype),
             pltpu.VMEM((2, n_z, chunk, width), wtype),
             dma((9,)),
+            dma((3,)),
         ]
         + [dma((2, n_z))] * 2
         + [dma((2,))] * 2
@@ -468,7 +504,7 @@
         + [dma((n_z,))] * 2
         + [dma(())] * 2,
         compiler_params=pltpu.CompilerParams(
-            collective_id=0, has_side_effects=True, vmem_limit_bytes=48 * 1024 * 1024
+            collective_id=0, has_side_effects=True, vmem_limit_bytes=62 * 1024 * 1024
         ),
         cost_estimate=pl.CostEstimate(
             flops=4 * targets * sources * width,
@@ -476,6 +512,15 @@
             transcendentals=share * width,
         ),
     )(*operands)
+    return pl.pallas_call(
+        hand_on,
+        out_shape=shapes,
+        in_specs=[hbm] * 3,
+        out_specs=(hbm,) * 3,
+        scratch_shapes=[pltpu.VMEM(item.shape, item.dtype) for item in shapes]
+        + [dma((3,))] * 2,
+        compiler_params=pltpu.CompilerParams(vmem_limit_bytes=62 * 1024 * 1024),
+    )(*results)
 
 
 def solution(mesh):

time: 46.9 us -> 41.6 us (0.89)
  local copies, waits for them, and re-layouts: 6.83 us -> 0 us
  Pallas kernels: 39.1 us -> 40.9 us
    unnamed x21 -> x0, local copies, waits for them, and re-layouts: 6.83 us -> none
    pallas_call x0 -> x1, Pallas kernels: none -> 1.79 us  [on_device(): pl.pallas_call(hand_on, out_shape=shapes, in_specs=[hbm] * 3, out_specs=(...]
where the time goes in v3:
time: 41.6 us; the launch traced here: 41.5 us
  Pallas kernels  40.9 us (98%)
  between operations  0.64 us (2%)
    pallas_call x1, Pallas kernels, on_device(): pl.pallas_call(functools.partial(kernel, n_row, n_col, targets * n_row),...  39.1 us
    pallas_call x1, Pallas kernels, on_device(): pl.pallas_call(hand_on, out_shape=shapes, in_specs=[hbm] * 3, out_specs=(...  1.79 us

profile of v3, /device:TPU:0, one launch (start us, length us, event | category | flops | bytes accessed | tf_op | source)
XLA Modules:
  0.0 41.5 jit_solution(1090397934300864367)
XLA Ops:
  0.6 39.1 %shard_map.112 = (bf16[256,256]{1,0:T(8,128)(2,1)}, f32[256,256]{1,0:T(8,128)}, bf16[128,256]{1,0:T(8,128)(2,1)}) custom-call(bf16[128,256]{1,0:T(8,128)(2,1)} %feat_hbm.1, f32[1,128]{1,0:T(1,128)} %bitcast.10, f32[8,128]{1,0:T(8,128)} %bitcast.8, bf16[256,256]{1,0:T(8,128)(2,1)} %weight_hbm.1, bf16[256,256]{1,0:T(8,128)(2,1)} %cot_hbm.1, s32[8,8]{1,0:T(8,128)} %bitcast.9, ...), custom_call_target="tpu_custom_call" | custom-call | flops 1073741824 | bytes 1048576 | tf_op jit(solution)/shard_map/pallas_call | solution.py:472
  39.7 1.8 %shard_map.113 = (bf16[256,256]{1,0:T(8,128)(2,1)}, f32[256,256]{1,0:T(8,128)}, bf16[128,256]{1,0:T(8,128)(2,1)}) custom-call(bf16[256,256]{1,0:T(8,128)(2,1)} %get-tuple-element.6.refs_0_, f32[256,256]{1,0:T(8,128)} %get-tuple-element.7.refs_1_, bf16[128,256]{1,0:T(8,128)(2,1)} %get-tuple-element.8.refs_2_), custom_call_target="tpu_custom_call" | custom-call | tf_op jit(solution)/shard_map/pallas_call | solution.py:515

commit v4 on v3

--- a/solution.py
+++ b/solution.py
@@ -81,6 +81,7 @@
     f_got,
     f_send,
     f_recv,
+    kept,
     w_pair,
     w_got,
     w_send,
@@ -341,9 +342,14 @@
     each(1, n_z, lambda step: w_copy(line_peer(step), level).start())
     w_recv[level] = w_send[level]
 
-    def f_pair_copy(part):
+    def f_pair_copy(part, at):
         return remote(
-            f_pair.at[part], f_got.at[part], fp_ss.at[part], fp_rs.at[part], other_row, col
+            f_pair.at[part, at],
+            f_got.at[part, at],
+            fp_ss.at[part, at],
+            fp_rs.at[part, at],
+            other_row,
+            col,
         )
 
     def f_copy(part, peer, at):
@@ -371,22 +377,37 @@
     for part in range(2):
         each(1, n_col, lambda step: gy_copy(part, col_peer(step), col_peer(step)).wait())
         grad_y = gy[part].reshape(n_col * share, half)
-        line = n_z * own
-        f_pair[part] = (
-            dot(adj_t[rows_at(1 - core, line), :], grad_y).reshape(n_z, own, half).astype(BF)
-        )
-        f_pair_copy(part).start()
-        kept = dot(adj_t[rows_at(core, line), :], grad_y).reshape(n_z, own, half)
+
+        def product(of_core, at):
+            return dot(adj_t[rows_at(of_core * n_z + at, own), :], grad_y)
+
+        def send_pair(step):
+            at = line_peer(step)
+            f_pair[part, at] = product(1 - core, at).astype(BF)
+            f_pair_copy(part, at).start()
+
+        def keep(step):
+            at = line_peer(step)
+            kept[at] = product(core, at)
+
+        def pass_on(step):
+            at = line_peer(step)
+            f_pair_copy(part, at).wait()
+            total = (kept[at] + f_got[part, at].astype(F32)).astype(BF)
+            f_send[part, at] = total
+            f_copy(part, at, level).start()
+
+        each(1, n_z + 1, send_pair)
+        each(1, n_z + 1, keep)
         if part == 1:
             each(1, n_col, lambda step: x_copy(col_peer(step), col_peer(step)).wait())
             w_all[core, level] = (
                 jnp.sum(x_all[...].astype(F32), axis=0) * (1.0 / math.sqrt(total_nodes))
             ).astype(w_all.dtype)
             each(1, n_z, lambda step: o_copy(line_peer(step), level).start())
-        f_pair_copy(part).wait()
-        f_send[part] = (kept + f_got[part].astype(F32)).astype(BF)
-        each(1, n_z, lambda step: f_copy(part, line_peer(step), level).start())
-        f_recv[part, level] = f_send[part, level]
+        each(1, n_z, pass_on)
+        f_pair_copy(part, level).wait()
+        f_recv[part, level] = (kept[level] + f_got[part, level].astype(F32)).astype(BF)
 
     def pair_o(of_core):
         return remote(w_all.at[of_core], w_all.at[of_core], op_ss, op_rs, other_row, col)
@@ -486,6 +507,7 @@
             pltpu.VMEM((2, n_col, share, half), BF),
         ]
         + [pltpu.VMEM((2, n_z, own, half), BF)] * 4
+        + [pltpu.VMEM((n_z, own, half), F32)]
         + [pltpu.VMEM((n_z, chunk, width), wtype)] * 4
         + [
             pltpu.VMEM((n_col, chunk, width), wtype),
@@ -496,7 +518,7 @@
         + [dma((2, n_z))] * 2
         + [dma((2,))] * 2
         + [dma((2, n_col))] * 4
-        + [dma((2,))] * 2
+        + [dma((2, n_z))] * 2
         + [dma((2, n_z))] * 2
         + [dma(())] * 2
         + [dma((n_z,))] * 2

time: 41.6 us -> 41.1 us (0.988)
  Pallas kernels: 40.9 us -> 40.3 us
    pallas_call x1, Pallas kernels: 39.1 us -> 38.5 us  [on_device(): pl.pallas_call(functools.partial(kernel, n_row, n_col, targets * n_row),...]
where the time goes in v4:
time: 41.1 us; the launch traced here: 40.9 us
  Pallas kernels  40.3 us (98%)
  between operations  0.64 us (2%)
    pallas_call x1, Pallas kernels, on_device(): pl.pallas_call(functools.partial(kernel, n_row, n_col, targets * n_row),...  38.5 us
    pallas_call x1, Pallas kernels, on_device(): pl.pallas_call(hand_on, out_shape=shapes, in_specs=[hbm] * 3, out_specs=(...  1.79 us

profile of v4, /device:TPU:0, one launch (start us, length us, event | category | flops | bytes accessed | tf_op | source)
XLA Modules:
  0.0 40.9 jit_solution(8467351250396222043)
XLA Ops:
  0.6 38.5 %shard_map.112 = (bf16[256,256]{1,0:T(8,128)(2,1)}, f32[256,256]{1,0:T(8,128)}, bf16[128,256]{1,0:T(8,128)(2,1)}) custom-call(bf16[128,256]{1,0:T(8,128)(2,1)} %feat_hbm.1, f32[1,128]{1,0:T(1,128)} %bitcast.10, f32[8,128]{1,0:T(8,128)} %bitcast.8, bf16[256,256]{1,0:T(8,128)(2,1)} %weight_hbm.1, bf16[256,256]{1,0:T(8,128)(2,1)} %cot_hbm.1, s32[8,8]{1,0:T(8,128)} %bitcast.9, ...), custom_call_target="tpu_custom_call" | custom-call | flops 1073741824 | bytes 1048576 | tf_op jit(solution)/shard_map/pallas_call | solution.py:493
  39.2 1.8 %shard_map.113 = (bf16[256,256]{1,0:T(8,128)(2,1)}, f32[256,256]{1,0:T(8,128)}, bf16[128,256]{1,0:T(8,128)(2,1)}) custom-call(bf16[256,256]{1,0:T(8,128)(2,1)} %get-tuple-element.6.refs_0_, f32[256,256]{1,0:T(8,128)} %get-tuple-element.7.refs_1_, bf16[128,256]{1,0:T(8,128)(2,1)} %get-tuple-element.8.refs_2_), custom_call_target="tpu_custom_call" | custom-call | tf_op jit(solution)/shard_map/pallas_call | solution.py:537
